TPU v7x, 512 devices: a whole 4x4x16 slice. The times are simulated.
512 devices in a mesh: dp: 64 (over y, z), tensor: 8 (over x, core).
Axes of the slice: x: 4, y: 4, z: 16, core: 2. Of those that a mesh axis runs over, the one named last changes fastest.
Arguments:
- layer_input: bfloat16 [24576, 4096], P(('dp', 'tensor')), may hold values from -1.5 to 1.5
- value_grad: bfloat16 [24576, 1024], P('dp', 'tensor'), may hold values from -1.1953125 to 1.1953125
- value_weight: bfloat16 [4096, 1024], P(None, 'tensor'), may hold values from -0.375 to 0.375
- error_buffer: bfloat16 [262144, 1024], P('dp', 'tensor'), may hold values from -6 to 6
- query_basis: float32 [1024, 32], P('tensor'), may hold values from -6 to 6
Outputs:
- input_grad: bfloat16 [24576, 4096], P(('dp', 'tensor'))
- error_new: bfloat16 [262144, 1024], P('dp', 'tensor')
- query_new: float32 [1024, 32], P('tensor')
All inputs are finite; a program needn't handle non-finite values.
Results may differ from a plain program's by a relative error of at most 0.017.
Values may be sent and summed in bfloat16 or wider, within the bound.
A program may use at most 64 MiB of HBM per device.

v0:
```python
import jax
import jax.numpy as jnp
from jax import lax
from jax.sharding import PartitionSpec as P


def per_device(layer_input, value_grad, value_weight, error_buffer, query_basis):
    replicas = lax.axis_size("dp")
    grad_rows = value_grad
    moment = lax.dot_general(
        lax.all_gather(layer_input, "tensor", axis=0, tiled=True),
        grad_rows,
        (((0,), (0,)), ((), ())),
        preferred_element_type=jnp.float32,
    )
    moment = moment + error_buffer.astype(jnp.float32)
    left_local = jnp.dot(
        moment, query_basis, precision=lax.Precision.HIGHEST, preferred_element_type=jnp.float32
    )
    left_sum = lax.psum(left_local, "dp") / replicas
    gram_matrix = jnp.dot(
        left_sum.T, left_sum, precision=lax.Precision.HIGHEST, preferred_element_type=jnp.float32
    )
    lower_factor = jnp.linalg.cholesky(gram_matrix)
    basis = lax.linalg.triangular_solve(
        lower_factor, left_sum, left_side=False, lower=True, transpose_a=True
    )
    right_local = lax.dot_general(
        moment,
        basis,
        (((0,), (0,)), ((), ())),
        precision=lax.Precision.HIGHEST,
        preferred_element_type=jnp.float32,
    )
    query_new = lax.psum(right_local, "dp") / replicas
    approx = jnp.dot(
        basis, query_new.T, precision=lax.Precision.HIGHEST, preferred_element_type=jnp.float32
    )
    error_new = (moment - approx).astype(jnp.bfloat16)
    grad_rows = value_grad
    summed = lax.psum_scatter(
        lax.dot_general(
            grad_rows, value_weight, (((1,), (1,)), ((), ())), preferred_element_type=jnp.float32
        ).astype(jnp.bfloat16),
        "tensor",
        scatter_dimension=0,
        tiled=True,
    )
    return (summed, error_new, query_new)


def solution(mesh):
    return jax.shard_map(
        per_device,
        mesh=mesh,
        in_specs=(
            P(("dp", "tensor"), None),
            P("dp", "tensor"),
            P(None, "tensor"),
            P("dp", "tensor"),
            P("tensor", None),
        ),
        out_specs=(P(("dp", "tensor"), None), P("dp", "tensor"), P("tensor", None)),
        check_vma=False,
    )
```

profile of v0, /device:TPU:4, one launch (start us, length us, event | category | flops | bytes accessed | tf_op | source)
XLA Modules:
  0.0 622.7 jit_solution(10687739770060608124)
XLA Ops:
  7.2 0.0 copy-start
  7.2 0.0 all-gather.2.cloned.1.call-start
  7.2 0.7 all-gather.2.cloned.1.call-update
  7.9 0.0 all-reduce.2.cloned.1.call-start
  8.0 40.8 %all-gather.2.cloned.1.call-done = bf16[384,4096]{1,0:T(8,128)(2,1)} async-done(((bf16[48,4096]{1,0:T(8,128)(2,1)}), bf16[384,4096]{1,0:T(8,128)(2,1)}) %all-gather.2.cloned.1.call-update) | async-done | bytes 3145744 | tf_op jit(solution)/shard_map/all_gather | solution.py:11
  48.8 3.3 convolution_add_fusion
  52.1 0.0 copy-start.2
  52.1 3.0 fusion.12
  55.1 0.0 all-reduce.2.cloned.1.call-update
  55.1 0.0 reduce-scatter.2.cloned.1.call-start
  55.1 2.6 convolution_convert_fusion
  57.8 0.0 reduce-scatter.2.cloned.1.call-update
  57.8 264.9 %all-reduce.2.cloned.1.call-done = f32[4096,32]{0,1:T(8,128)} async-done(((f32[4096,32]{0,1:T(8,128)}), f32[4096,32]{0,1:T(8,128)}) %all-reduce.2.cloned.1.call-update) | async-done | bytes 524304 | tf_op jit(solution)/shard_map/psum | solution.py:20
  322.7 1.8 fusion.3
  324.5 0.1 copy.8
  324.6 2.9 cholesky.16
  327.5 0.6 compare_reduce_fusion
  328.2 0.7 fusion.7
  328.8 2.4 custom-call.6
  331.3 1.7 fusion.1
  333.0 0.8 copy-done.1
  333.8 1.3 fusion.13
  335.1 275.6 %psum.15 = f32[128,32]{0,1:T(8,128)S(1)} all-reduce(f32[128,32]{0,1:T(8,128)S(1)} %fusion.13), channel_id=1, replica_groups=mesh['dp'=64,'tensor'=8] {'dp'}, use_global_device_ids=true, to_apply=%region_4.5 | all-reduce | flops 4096 | bytes 32768 | tf_op jit(solution)/shard_map/psum | solution.py:35
  610.7 5.5 fusion
  (11 shorter events, 0.1 us)
Async XLA Ops:
  7.2 48.0 %copy-start = (bf16[4096,128]{1,0:T(8,128)(2,1)S(1)}, bf16[4096,128]{1,0:T(8,128)(2,1)}, u32[]{:S(2)}) copy-start(bf16[4096,128]{1,0:T(8,128)(2,1)} %param.7) | copy-start | bytes 3145732
  7.2 41.6 %all-gather.2.cloned.1.call-start = ((), (), s32[]{:S(2)}) async-start(), calls=%async_computation.2 | async-start | bytes 3538944 | tf_op jit(solution)/shard_map/all_gather | solution.py:11
  7.9 44.1 %copy-start.4 = (f32[128,32]{0,1:T(8,128)S(1)}, f32[128,32]{0,1:T(8,128)}, u32[]{:S(2)}) copy-start(f32[128,32]{0,1:T(8,128)} %param.9) | copy-start | bytes 49156
  7.9 314.8 %all-reduce.2.cloned.1.call-start = ((), (), s32[]{:S(2)}) async-start(), calls=%async_computation.3 | async-start | bytes 1048576 | tf_op jit(solution)/shard_map/psum | solution.py:20
  52.1 3.1 copy-start.2
  55.1 561.1 %reduce-scatter.2.cloned.1.call-start = ((), (), s32[]{:S(2)}) async-start(), calls=%async_computation.1 | async-start | bytes 3538944 | tf_op jit(solution)/shard_map/reduce_scatter | solution.py:41
  333.0 0.8 copy-start.1
  610.7 5.5 copy-start.3
Sparse Core Ops, SparseCore 0:
  10.1 38.6 all-gather.1
  55.2 267.4 all-reduce.1
  326.4 32.9 reduce-scatter.1
where the time goes:
time: 623 us
  waiting for transfers between devices  306 us (49%)
  blocking collectives  276 us (44%)
  matrix products  19.1 us (3%)
  between operations  13.8 us (2%)
  other arithmetic  6.69 us (1%)
    psum x1, blocking collectives, per_device(): query_new = lax.psum(right_local, 'dp') / replicas  276 us
    psum x1, waiting for transfers between devices, per_device(): left_sum = lax.psum(left_local, 'dp') / replicas  265 us
    all_gather x1, waiting for transfers between devices, per_device(): lax.all_gather(layer_input, 'tensor', axis=0, tiled=True)  40.8 us
  transfers between devices with their start and end apart: 3, of which 2 were waited for; matrix products, arithmetic and copies ran while one was open for 3% of the time, Pallas kernels for 0%

commit v1 on v0

v1 whole, which is shorter than its diff:
```python
import functools

import jax
import jax.numpy as jnp
from jax import lax
from jax.experimental import pallas as pl
from jax.experimental.pallas import tpu as pltpu
from jax.sharding import PartitionSpec as P

MESH = pl.DeviceIdType.MESH
F32 = jnp.float32
BF16 = jnp.bfloat16
NY, NZ, NX, NCORE = 4, 16, 4, 2
NT = NX * NCORE
NC = 4


def dot_rows(a, b):
    return lax.dot_general(a, b, (((0,), (0,)), ((), ())), preferred_element_type=F32)


def moment_kernel(
    x_ref, g_ref, e_ref, mom_ref, mean_ref,
    xg, ystage, yrecv, zsum, zstage, zrecv,
    x_send, x_recv, c_send, c_recv, ys_send, ys_recv, zs_send, zs_recv,
    zg_send, zg_recv, yg_send, yg_recv, own_sem,
):
    r, t = lax.axis_index("dp"), lax.axis_index("tensor")
    y, z = r // NZ, lax.rem(r, NZ)
    x, core = t // NCORE, lax.rem(t, NCORE)
    rows, width = x_ref.shape
    ck = width // NC
    py = ck // NY
    pz = py // NZ

    def at_y(d):
        return (lax.rem(y + d, NY) * NZ + z, t)

    def at_z(d):
        return (y * NZ + lax.rem(z + d, NZ), t)

    def at_x(d):
        return (r, lax.rem(x + d, NX) * NCORE + core)

    sibling = (r, x * NCORE + 1 - core)

    barrier = pltpu.get_barrier_semaphore()
    peers = [sibling] + [at_x(d) for d in range(1, NX)] + [at_y(d) for d in range(1, NY)]
    for peer in peers:
        pl.semaphore_signal(barrier, inc=1, device_id=peer, device_id_type=MESH)

    def greet(d, carry):
        pl.semaphore_signal(barrier, inc=1, device_id=at_z(d), device_id_type=MESH)
        return carry

    lax.fori_loop(1, NZ, greet, 0)
    pl.semaphore_wait(barrier, len(peers) + NZ - 1)

    def block(c, owner):
        return xg.at[c, pl.ds(pl.multiple_of(owner * rows, rows), rows)]

    def owner_x(d):
        return lax.rem(x + d, NX) * NCORE + core

    own = []
    sends = []
    for c in range(NC):
        src = x_ref.at[:, pl.ds(c * ck, ck)]
        local = pltpu.make_async_copy(src, block(c, t), own_sem.at[c])
        local.start()
        own.append(local)
        for d in range(1, NX):
            cp = pltpu.make_async_remote_copy(
                src, block(c, t), x_send.at[c, d - 1], x_recv.at[c, d - 1],
                device_id=at_x(d), device_id_type=MESH,
            )
            cp.start()
            sends.append(cp)
        cp = pltpu.make_async_remote_copy(
            src, block(c, t), c_send.at[c, 0], c_recv.at[c, 0],
            device_id=sibling, device_id_type=MESH,
        )
        cp.start()
        sends.append(cp)

    def wait_bytes(ref, sem):
        pltpu.make_async_copy(ref, ref, sem).wait()

    def forward(c):
        for d in range(1, NX):
            got = block(c, owner_x(NX - d))
            wait_bytes(got, x_recv.at[c, d - 1])
            cp = pltpu.make_async_remote_copy(
                got, got, c_send.at[c, d], c_recv.at[c, d],
                device_id=sibling, device_id_type=MESH,
            )
            cp.start()
            sends.append(cp)

    def moment(c):
        own[c].wait()
        for d in range(NX):
            wait_bytes(block(c, t), c_recv.at[c, d])
        def tile(j, carry):
            off = pl.multiple_of(j * py, py)
            at = pl.multiple_of(c * ck + j * py, py)
            m = dot_rows(xg[c, :, pl.ds(off, py)], g_ref[...])
            m = m + e_ref[pl.ds(at, py), :].astype(F32)
            mom_ref[pl.ds(at, py), :] = m
            ystage[c, j] = m.astype(BF16)
            return carry
        lax.fori_loop(0, NY, tile, 0)
        for d in range(1, NY):
            cp = pltpu.make_async_remote_copy(
                ystage.at[c, lax.rem(y + d, NY)], yrecv.at[c, d - 1],
                ys_send.at[c, d - 1], ys_recv.at[c, d - 1],
                device_id=at_y(d), device_id_type=MESH,
            )
            cp.start()
            sends.append(cp)

    def z_scatter(c):
        for d in range(1, NY):
            wait_bytes(yrecv.at[c, d - 1], ys_recv.at[c, d - 1])
        total = mom_ref[pl.ds(pl.multiple_of(c * ck + y * py, py), py), :]
        for d in range(1, NY):
            total = total + yrecv[c, d - 1].astype(F32)
        zsum[c] = total
        zstage[c] = total.astype(BF16)

        def send(d, carry):
            at = pl.multiple_of(lax.rem(z + d, NZ) * pz, pz)
            pltpu.make_async_remote_copy(
                zstage.at[c, pl.ds(at, pz)], zrecv.at[c, d - 1],
                zs_send.at[c], zs_recv.at[c],
                device_id=at_z(d), device_id_type=MESH,
            ).start()
            return carry

        lax.fori_loop(1, NZ, send, 0)

    def z_gather(c):
        wait_bytes(zrecv.at[c], zs_recv.at[c])
        total = zsum[c, pl.ds(pl.multiple_of(z * pz, pz), pz), :]
        for d in range(1, NZ):
            total = total + zrecv[c, d - 1].astype(F32)
        at = pl.multiple_of(c * ck + y * py + z * pz, pz)
        mine = mean_ref.at[pl.ds(at, pz)]
        mine[...] = (total * (1.0 / (NY * NZ))).astype(BF16)

        def send(d, carry):
            pltpu.make_async_remote_copy(
                mine, mine, zg_send.at[c], zg_recv.at[c],
                device_id=at_z(d), device_id_type=MESH,
            ).start()
            return carry

        lax.fori_loop(1, NZ, send, 0)

    def y_gather(c):
        at = pl.multiple_of(c * ck + y * py, py)
        wait_bytes(mean_ref.at[pl.ds(at, py - pz)], zg_recv.at[c])
        mine = mean_ref.at[pl.ds(at, py)]
        for d in range(1, NY):
            cp = pltpu.make_async_remote_copy(
                mine, mine, yg_send.at[c, d - 1], yg_recv.at[c, d - 1],
                device_id=at_y(d), device_id_type=MESH,
            )
            cp.start()
            sends.append(cp)

    def finish(c):
        at = pl.multiple_of(c * ck + y * py, py)
        for d in range(1, NY):
            wait_bytes(mean_ref.at[pl.ds(at, py)], yg_recv.at[c, d - 1])

    stages = [(forward, 0.0), (moment, 1.0), (z_scatter, 6.5), (z_gather, 15.0), (y_gather, 24.0), (finish, 30.0)]
    order = sorted(
        ((4.2 * c + at, i, c, fn) for i, (fn, at) in enumerate(stages) for c in range(NC)),
        key=lambda e: e[:3],
    )
    for _, _, c, fn in order:
        fn(c)

    for cp in sends:
        cp.wait_send()
    for c in range(NC):
        wait_bytes(zrecv.at[c], zs_send.at[c])
        wait_bytes(zrecv.at[c], zg_send.at[c])


def reduce_moment(layer_input, value_grad, error_buffer):
    rows, width = layer_input.shape
    tokens, head = value_grad.shape
    ck = width // NC
    py = ck // NY
    pz = py // NZ
    dma = pltpu.SemaphoreType.DMA
    vmem = pl.BlockSpec(memory_space=pltpu.VMEM)
    return pl.pallas_call(
        moment_kernel,
        out_shape=(
            jax.ShapeDtypeStruct((width, head), F32),
            jax.ShapeDtypeStruct((width, head), BF16),
        ),
        in_specs=[vmem] * 3,
        out_specs=(vmem, vmem),
        scratch_shapes=[
            pltpu.VMEM((NC, tokens, ck), BF16),
            pltpu.VMEM((NC, NY, py, head), BF16),
            pltpu.VMEM((NC, NY - 1, py, head), BF16),
            pltpu.VMEM((NC, py, head), F32),
            pltpu.VMEM((NC, py, head), BF16),
            pltpu.VMEM((NC, NZ - 1, pz, head), BF16),
            dma((NC, NX - 1)), dma((NC, NX - 1)),
            dma((NC, NX)), dma((NC, NX)),
            dma((NC, NY - 1)), dma((NC, NY - 1)),
            dma((NC,)), dma((NC,)),
            dma((NC,)), dma((NC,)),
            dma((NC, NY - 1)), dma((NC, NY - 1)),
            dma((NC,)),
        ],
        compiler_params=pltpu.CompilerParams(
            collective_id=0, has_side_effects=True, vmem_limit_bytes=40 * 2**20
        ),
        name="reduce_moment",
    )(layer_input, value_grad, error_buffer)


def high(a, b):
    return jnp.dot(a, b, precision=lax.Precision.HIGHEST, preferred_element_type=F32)


def finish_kernel(mom_ref, mean_ref, q_ref, err_ref, qn_ref):
    width, head = mean_ref.shape
    rank = q_ref.shape[1]
    tile = 512

    def gram(j, acc):
        m = mean_ref[pl.ds(pl.multiple_of(j * tile, tile), tile), :]
        return acc + dot_rows(m, m)

    k = lax.fori_loop(0, width // tile, gram, jnp.zeros((head, head), F32))
    q = q_ref[...]
    right = high(q.T, k)
    s = high(right, q)
    row_of = lax.broadcasted_iota(jnp.int32, (rank, 1), 0)
    out = jnp.zeros((rank, head), F32)
    for i in range(rank):
        pivot = s[i:i + 1, i:i + 1]
        inv = 1.0 / pivot
        srow = s[i:i + 1, :] * inv
        rrow = right[i:i + 1, :] * inv
        mine = row_of == i
        out = jnp.where(mine, rrow * jnp.sqrt(pivot), out)
        col = jnp.where(mine, 0.0, s[:, i:i + 1])
        s = jnp.where(mine, srow, s - col * srow)
        right = jnp.where(mine, rrow, right - col * rrow)
    qn_ref[...] = out.T
    b = high(q, right)
    b_hi = b.astype(BF16)
    b_lo = (b - b_hi.astype(F32)).astype(BF16)

    def error(j, carry):
        at = pl.ds(pl.multiple_of(j * tile, tile), tile)
        m = mean_ref[at, :]
        approx = jnp.dot(m, b_hi, preferred_element_type=F32) + jnp.dot(m, b_lo, preferred_element_type=F32)
        err_ref[at, :] = (mom_ref[at, :] - approx).astype(BF16)
        return carry

    lax.fori_loop(0, width // tile, error, 0)


def finish(mom, mean, query_basis):
    vmem = pl.BlockSpec(memory_space=pltpu.VMEM)
    return pl.pallas_call(
        finish_kernel,
        out_shape=(
            jax.ShapeDtypeStruct(mean.shape, BF16),
            jax.ShapeDtypeStruct(query_basis.shape, F32),
        ),
        in_specs=[vmem] * 3,
        out_specs=(vmem, vmem),
        compiler_params=pltpu.CompilerParams(vmem_limit_bytes=32 * 2**20),
        name="finish",
    )(mom, mean, query_basis)


def per_device(layer_input, value_grad, value_weight, error_buffer, query_basis):
    term = lax.dot_general(
        value_grad, value_weight, (((1,), (1,)), ((), ())), preferred_element_type=F32
    ).astype(BF16)
    summed = lax.psum_scatter(term, "tensor", scatter_dimension=0, tiled=True)
    mom, mean = reduce_moment(layer_input, value_grad, error_buffer)
    error_new, query_new = finish(mom, mean, query_basis)
    return (summed, error_new, query_new)


def solution(mesh):
    return jax.shard_map(
        per_device,
        mesh=mesh,
        in_specs=(
            P(("dp", "tensor"), None),
            P("dp", "tensor"),
            P(None, "tensor"),
            P("dp", "tensor"),
            P("tensor", None),
        ),
        out_specs=(P(("dp", "tensor"), None), P("dp", "tensor"), P("tensor", None)),
        check_vma=False,
    )
```

time: 623 us -> 102 us (0.16)
  the two profiles are of different devices: /device:TPU:4 before, /device:TPU:1 now
where the time goes in v1:
time: 102 us
  Pallas kernels  81.9 us (80%)
  between operations  14.1 us (14%)
  matrix products  3.52 us (3%)
  local copies, waits for them, and re-layouts  1.95 us (2%)
    pallas_call x1, Pallas kernels, reduce_moment(): pl.pallas_call(moment_kernel, out_shape=(jax.ShapeDtypeStruct((width, hea...  74 us
    pallas_call x1, Pallas kernels, finish(): pl.pallas_call(finish_kernel, out_shape=(jax.ShapeDtypeStruct(mean.shape,...  7.87 us
    dot_general x1, matrix products, per_device(): lax.dot_general(value_grad, value_weight, (((1,), (1,)), ((), ())), prefe...  3.52 us
  transfers between devices with their start and end apart: 1, of which 0 were waited for; matrix products, arithmetic and copies ran while one was open for 1% of the time, Pallas kernels for 81%

profile of v1, /device:TPU:1, one launch (start us, length us, event | category | flops | bytes accessed | tf_op | source)
XLA Modules:
  0.0 101.5 jit_solution(17258169769130018008)
XLA Ops:
  7.2 0.0 copy-start
  7.2 0.0 copy-start.3
  7.2 0.0 copy-start.4
  7.2 0.0 copy-start.2
  7.2 0.0 copy-start.1
  7.2 0.0 reduce-scatter.2.cloned.1.call-start
  7.3 1.1 %copy-done = bf16[4096,128]{1,0:T(8,128)(2,1)S(1)} copy-done((bf16[4096,128]{1,0:T(8,128)(2,1)S(1)}, bf16[4096,128]{1,0:T(8,128)(2,1)}, u32[]{:S(2)}) %copy-start) | copy-done | bytes 1048600
  8.4 3.5 %convolution_convert_fusion = bf16[384,4096]{1,0:T(8,128)(2,1)} fusion(bf16[384,128]{1,0:T(8,128)(2,1)} %g_ref.1, bf16[4096,128]{1,0:T(8,128)(2,1)S(1)} %copy-done), kind=kOutput, calls=%fused_computation | convolution fusion | flops 404226048 | bytes 4292608 | tf_op jit(solution)/shard_map/dot_general | solution.py:290
  11.9 0.0 reduce-scatter.2.cloned.1.call-update
  12.0 0.0 copy-done.4
  12.0 0.1 copy.8.q_ref
  12.1 0.0 copy-done.3
  12.1 0.0 copy-done.2
  12.1 0.0 copy-done.1
  12.1 74.0 %reduce_moment.1 = (f32[4096,128]{1,0:T(8,128)S(1)}, bf16[4096,128]{1,0:T(8,128)(2,1)S(1)}) custom-call(bf16[48,4096]{1,0:T(8,128)(2,1)S(1)} %copy-done.2, bf16[384,128]{1,0:T(8,128)(2,1)S(1)} %copy-done.3, bf16[4096,128]{1,0:T(8,128)(2,1)S(1)} %copy-done.1), custom_call_target="tpu_custom_call" | custom-call | tf_op jit(solution)/shard_map/reduce_moment/pallas_call | solution.py:200
  86.1 7.9 %finish.1 = (bf16[4096,128]{1,0:T(8,128)(2,1)}, f32[128,32]{1,0:T(8,128)S(1)}) custom-call(f32[4096,128]{1,0:T(8,128)S(1)} %get-tuple-element.7.mom_ref, bf16[4096,128]{1,0:T(8,128)(2,1)S(1)} %get-tuple-element.8.mean_ref, f32[128,32]{1,0:T(8,128)S(1)} %copy.8.q_ref), custom_call_target="tpu_custom_call" | custom-call | tf_op jit(solution)/shard_map/finish/pallas_call | solution.py:276
  94.0 0.7 copy.9
  94.7 0.0 reduce-scatter.2.cloned.1.call-done
Async XLA Ops:
  7.2 1.2 %copy-start = (bf16[4096,128]{1,0:T(8,128)(2,1)S(1)}, bf16[4096,128]{1,0:T(8,128)(2,1)}, u32[]{:S(2)}) copy-start(bf16[4096,128]{1,0:T(8,128)(2,1)} %param.7) | copy-start | bytes 3145732
  7.2 4.9 %copy-start.3 = (bf16[384,128]{1,0:T(8,128)(2,1)S(1)}, bf16[384,128]{1,0:T(8,128)(2,1)}, u32[]{:S(2)}) copy-start(bf16[384,128]{1,0:T(8,128)(2,1)} %g_ref.1) | copy-start | bytes 294916
  7.2 4.8 %copy-start.4 = (f32[128,32]{0,1:T(8,128)S(1)}, f32[128,32]{0,1:T(8,128)}, u32[]{:S(2)}) copy-start(f32[128,32]{0,1:T(8,128)} %param.9) | copy-start | bytes 49156
  7.2 4.9 %copy-start.2 = (bf16[48,4096]{1,0:T(8,128)(2,1)S(1)}, bf16[48,4096]{1,0:T(8,128)(2,1)}, u32[]{:S(2)}) copy-start(bf16[48,4096]{1,0:T(8,128)(2,1)} %x_ref.1) | copy-start | bytes 1179652
  7.2 4.9 %copy-start.1 = (bf16[4096,128]{1,0:T(8,128)(2,1)S(1)}, bf16[4096,128]{1,0:T(8,128)(2,1)}, u32[]{:S(2)}) copy-start(bf16[4096,128]{1,0:T(8,128)(2,1)} %e_ref.1) | copy-start | bytes 3145732
  7.2 87.5 %reduce-scatter.2.cloned.1.call-start = ((), (), s32[]{:S(2)}) async-start(), calls=%async_computation.1 | async-start | bytes 3538944 | tf_op jit(solution)/shard_map/reduce_scatter | solution.py:293
Sparse Core Ops, SparseCore 0:
  12.1 55.2 reduce-scatter.1

commit v2 on v1

v2 whole, which is shorter than its diff:
```python
import functools

import jax
import jax.numpy as jnp
from jax import lax
from jax.experimental import pallas as pl
from jax.experimental.pallas import tpu as pltpu
from jax.sharding import PartitionSpec as P

MESH = pl.DeviceIdType.MESH
F32 = jnp.float32
BF16 = jnp.bfloat16
NY, NZ, NX, NCORE = 4, 16, 4, 2
NT = NX * NCORE
NC = 4
AHEAD = 2
FAR_FIRST = sorted(range(1, NZ), key=lambda d: -min(d, NZ - d))


def dot_rows(a, b):
    return lax.dot_general(a, b, (((0,), (0,)), ((), ())), preferred_element_type=F32)


def high(a, b, dims):
    return lax.dot_general(
        a, b, (dims, ((), ())), precision=lax.Precision.HIGHEST, preferred_element_type=F32
    )


def kernel(
    x_hbm, g_hbm, w_hbm, e_hbm, q_ref,
    ig_hbm, err_hbm, qn_ref,
    g_ref, w_ref, e_ref,
    xg, mom_ref, mean_ref, ystage, yrecv, zsum, zstage, zrecv, gram_ref,
    term, other, pair, pair_recv, home, ig_ref, err_ref,
    out_sem, load_sem, entered,
    x_send, x_recv, c_send, c_recv, ys_send, ys_recv, zs_send, zs_recv,
    zg_send, zg_recv, yg_send, yg_recv, t_send, t_recv, p_send, p_recv, own_sem,
):
    r, t = lax.axis_index("dp"), lax.axis_index("tensor")
    y, z = r // NZ, lax.rem(r, NZ)
    x, core = t // NCORE, lax.rem(t, NCORE)
    rows, width = x_hbm.shape
    tokens, head = g_hbm.shape
    rank = q_ref.shape[0]
    ck = width // NC
    py = ck // NY
    pz = py // NZ
    wide = 512

    def at_y(d):
        return (lax.rem(y + d, NY) * NZ + z, t)

    def at_z(d):
        return (y * NZ + lax.rem(z + d, NZ), t)

    def owner_x(d, c):
        return lax.rem(x + d, NX) * NCORE + c

    def at_x(d):
        return (r, owner_x(d, core))

    sibling = (r, x * NCORE + 1 - core)

    barrier = pltpu.get_barrier_semaphore()
    peers = [at_x(1), at_x(3), sibling, at_x(2), at_z(1), at_z(NZ - 1), at_y(1), at_y(3), at_y(2)]
    for peer in peers:
        pl.semaphore_signal(barrier, inc=1, device_id=peer, device_id_type=MESH)

    loads = [
        pltpu.make_async_copy(src, dst, load_sem.at[i])
        for i, (src, dst) in enumerate(((g_hbm, g_ref), (w_hbm, w_ref), (e_hbm, e_ref)))
    ]
    for cp in loads:
        cp.start()

    def block(c, owner, part=slice(None)):
        return xg.at[c, pl.ds(pl.multiple_of(owner * rows, rows), rows), part]

    own = []
    for c in range(NC):
        own.append(pltpu.make_async_copy(x_hbm.at[:, pl.ds(c * ck, ck)], block(c, t), own_sem.at[c]))
        own[c].start()
    pl.semaphore_wait(barrier, len(peers))

    sends = []

    def remote(src, dst, send, recv, device):
        cp = pltpu.make_async_remote_copy(
            src, dst, send, recv, device_id=device, device_id_type=MESH
        )
        cp.start()
        sends.append(cp)

    def spread(c):
        src = x_hbm.at[:, pl.ds(c * ck, ck)]
        remote(src, block(c, t), x_send.at[c, 0], x_recv.at[c, 0], at_x(1))
        remote(src, block(c, t), x_send.at[c, 1], x_recv.at[c, 1], at_x(3))
        remote(src, block(c, t), c_send.at[c, 0], c_recv.at[c, 0], sibling)

    def greet(i):
        if i > 0:
            pl.semaphore_wait(entered.at[i - 1], 2)
        if i < 3:
            for d in (2**i, NZ - 2**i):
                pl.semaphore_signal(entered.at[i], inc=1, device_id=at_z(d), device_id_type=MESH)

    def row_block(ref, owner):
        return ref.at[pl.ds(pl.multiple_of(owner * rows, rows), rows)]

    def head_term(c):
        if c == 0:
            loads[1].wait()

        def tile(j, carry):
            at = pl.ds(pl.multiple_of(j * wide, wide), wide)
            term[:, at] = lax.dot_general(
                g_ref[...], w_ref[at, :], (((1,), (1,)), ((), ())), preferred_element_type=F32
            ).astype(BF16)
            return carry

        half = width // wide // 2
        lax.fori_loop(c * half, (c + 1) * half, tile, 0)
        if c == 0:
            return
        for d in range(NX):
            remote(
                row_block(term, owner_x(d, 1 - core)), other.at[d],
                t_send.at[d], t_recv.at[d], sibling,
            )

    def wait_bytes(ref, sem):
        pltpu.make_async_copy(ref, ref, sem).wait()

    left, right = pl.ds(0, ck // 2), pl.ds(ck // 2, ck // 2)

    def forward(c):
        for i, (d, part, to) in enumerate(((3, left, 1), (1, right, 3))):
            owner = owner_x(d, core)
            got = block(c, owner)
            wait_bytes(got, x_recv.at[c, i])
            half = block(c, owner, part)
            remote(half, half, x_send.at[c, 2 + i], x_recv.at[c, 2 + i], at_x(to))
            remote(got, got, c_send.at[c, 1 + i], c_recv.at[c, 1 + i], sibling)
        if c + AHEAD < NC:
            spread(c + AHEAD)

    def forward_far(c):
        owner = owner_x(2, core)
        wait_bytes(block(c, owner, left), x_recv.at[c, 2])
        wait_bytes(block(c, owner, right), x_recv.at[c, 3])
        got = block(c, owner)
        remote(got, got, c_send.at[c, 3], c_recv.at[c, 3], sibling)

    def moment(c):
        own[c].wait()
        if c == 0:
            loads[0].wait()
            loads[2].wait()
        for d in range(NX):
            wait_bytes(block(c, t), c_recv.at[c, d])

        def tile(j, carry):
            off = pl.multiple_of(j * py, py)
            at = pl.multiple_of(c * ck + j * py, py)
            m = dot_rows(xg[c, :, pl.ds(off, py)], g_ref[...])
            m = m + e_ref[pl.ds(at, py), :].astype(F32)
            mom_ref[pl.ds(at, py), :] = m
            ystage[c, j] = m.astype(BF16)
            return carry

        lax.fori_loop(0, NY, tile, 0)
        for d in (1, 3, 2):
            remote(
                ystage.at[c, lax.rem(y + d, NY)], yrecv.at[c, d - 1],
                ys_send.at[c, d - 1], ys_recv.at[c, d - 1], at_y(d),
            )

    def z_scatter(c):
        for d in range(1, NY):
            wait_bytes(yrecv.at[c, d - 1], ys_recv.at[c, d - 1])
        total = mom_ref[pl.ds(pl.multiple_of(c * ck + y * py, py), py), :]
        for d in range(1, NY):
            total = total + yrecv[c, d - 1].astype(F32)
        zsum[c] = total
        zstage[c] = total.astype(BF16)

        for d in FAR_FIRST:
            at = pl.multiple_of(lax.rem(z + d, NZ) * pz, pz)
            pltpu.make_async_remote_copy(
                zstage.at[c, pl.ds(at, pz)], zrecv.at[c, d - 1],
                zs_send.at[c], zs_recv.at[c],
                device_id=at_z(d), device_id_type=MESH,
            ).start()

    def z_gather(c):
        wait_bytes(zrecv.at[c], zs_recv.at[c])
        total = zsum[c, pl.ds(pl.multiple_of(z * pz, pz), pz), :]
        for d in range(1, NZ):
            total = total + zrecv[c, d - 1].astype(F32)
        at = pl.multiple_of(c * ck + y * py + z * pz, pz)
        mine = mean_ref.at[pl.ds(at, pz)]
        mine[...] = (total * (1.0 / (NY * NZ))).astype(BF16)

        for d in FAR_FIRST:
            pltpu.make_async_remote_copy(
                mine, mine, zg_send.at[c], zg_recv.at[c],
                device_id=at_z(d), device_id_type=MESH,
            ).start()

    def y_gather(c):
        at = pl.multiple_of(c * ck + y * py, py)
        wait_bytes(mean_ref.at[pl.ds(at, py - pz)], zg_recv.at[c])
        mine = mean_ref.at[pl.ds(at, py)]
        for d in (1, 3, 2):
            remote(mine, mine, yg_send.at[c, d - 1], yg_recv.at[c, d - 1], at_y(d))

    def gram(c):
        at = pl.multiple_of(c * ck + y * py, py)
        for d in range(1, NY):
            wait_bytes(mean_ref.at[pl.ds(at, py)], yg_recv.at[c, d - 1])
        m = mean_ref[pl.ds(c * ck, ck), :]
        part = dot_rows(m, m)
        gram_ref[...] = part if c == 0 else gram_ref[...] + part

    def pair_sum(c):
        for d in range(NX):
            wait_bytes(other.at[d], t_recv.at[d])
        for d in range(NX):
            mine = row_block(term, owner_x(d, core))

            def tile(j, carry):
                at = pl.ds(pl.multiple_of(j * wide, wide), wide)
                both = mine[:, at].astype(F32) + other[d, :, at].astype(F32)
                if d == 0:
                    home[:, at] = both
                else:
                    pair[d - 1, :, at] = both.astype(BF16)
                return carry

            lax.fori_loop(0, width // wide, tile, 0)

    def pair_send(c):
        for d in (1, 3, 2):
            remote(pair.at[d - 1], pair_recv.at[d - 1], p_send.at[d - 1], p_recv.at[d - 1], at_x(d))

    stores = []

    def store(src, dst):
        cp = pltpu.make_async_copy(src, dst, out_sem.at[len(stores)])
        cp.start()
        stores.append(cp)

    def input_grad(c):
        for d in range(1, NX):
            wait_bytes(pair_recv.at[d - 1], p_recv.at[d - 1])

        def tile(j, carry):
            at = pl.ds(pl.multiple_of(j * wide, wide), wide)
            total = home[:, at]
            for d in range(1, NX):
                total = total + pair_recv[d - 1, :, at].astype(F32)
            ig_ref[:, at] = total.astype(BF16)
            return carry

        lax.fori_loop(0, width // wide, tile, 0)
        store(ig_ref, ig_hbm)

    stages = [
        (forward, 4.5), (forward_far, 8.7), (moment, 9.7), (z_scatter, 15.2), (z_gather, 24.0),
        (y_gather, 33.5), (gram, 39.0),
    ]
    order = [(2.6 * c + at, i, c, fn) for i, (fn, at) in enumerate(stages) for c in range(NC)]
    order += [
        (0.0, 0, 0, greet), (18.0, 0, 0, head_term), (3.0, 0, 1, greet), (18.5, 0, 1, head_term),
        (6.0, 0, 2, greet), (13.0, 0, 3, greet),
        (21.0, 9, 0, pair_sum), (21.1, 9, 0, pair_send), (40.0, 9, 0, input_grad),
    ]
    for c in range(AHEAD):
        spread(c)
    for _, _, c, fn in sorted(order, key=lambda e: e[:3]):
        fn(c)

    q = q_ref[...]
    prod = high(q, gram_ref[...], ((1,), (0,)))
    s = high(prod, q, ((1,), (1,)))
    row_of = lax.broadcasted_iota(jnp.int32, (rank, 1), 0)
    out = jnp.zeros((rank, head), F32)
    for i in range(rank):
        pivot = s[i:i + 1, i:i + 1]
        inv = 1.0 / pivot
        srow = s[i:i + 1, :] * inv
        rrow = prod[i:i + 1, :] * inv
        mine = row_of == i
        out = jnp.where(mine, rrow * jnp.sqrt(pivot), out)
        col = jnp.where(mine, 0.0, s[:, i:i + 1])
        s = jnp.where(mine, srow, s - col * srow)
        prod = jnp.where(mine, rrow, prod - col * rrow)
    qn_ref[...] = out
    b = high(q, prod, ((0,), (0,)))
    b_hi = b.astype(BF16)
    b_both = jnp.concatenate([b_hi, (b - b_hi.astype(F32)).astype(BF16)], axis=0)

    for j in range(width // wide):
        at = pl.ds(j * wide, wide)
        m = mean_ref[at, :]
        approx = jnp.dot(jnp.concatenate([m, m], axis=1), b_both, preferred_element_type=F32)
        err_ref[at, :] = (mom_ref[at, :] - approx).astype(BF16)
        store(err_ref.at[at], err_hbm.at[at])

    for cp in stores:
        cp.wait()
    for cp in sends:
        cp.wait_send()
    for c in range(NC):
        wait_bytes(zrecv.at[c], zs_send.at[c])
        wait_bytes(zrecv.at[c], zg_send.at[c])


def deliver_kernel(*refs):
    n = len(refs) // 2
    for src, dst in zip(refs[:n], refs[n:]):
        dst[...] = src[...]


def deliver(*arrays):
    vmem = pl.BlockSpec(memory_space=pltpu.VMEM)
    return pl.pallas_call(
        deliver_kernel,
        out_shape=tuple(jax.ShapeDtypeStruct(a.shape, a.dtype) for a in arrays),
        in_specs=[vmem] * len(arrays),
        out_specs=(vmem,) * len(arrays),
        compiler_params=pltpu.CompilerParams(vmem_limit_bytes=56 * 2**20),
        name="deliver",
    )(*arrays)


def per_device(layer_input, value_grad, value_weight, error_buffer, query_basis):
    rows, width = layer_input.shape
    tokens, head = value_grad.shape
    rank = query_basis.shape[1]
    ck = width // NC
    py = ck // NY
    pz = py // NZ
    dma = pltpu.SemaphoreType.DMA
    vmem = pl.BlockSpec(memory_space=pltpu.VMEM)
    hbm = pl.BlockSpec(memory_space=pltpu.HBM)
    input_grad, error_new, query_new = pl.pallas_call(
        kernel,
        out_shape=(
            jax.ShapeDtypeStruct((rows, width), BF16),
            jax.ShapeDtypeStruct((width, head), BF16),
            jax.ShapeDtypeStruct((rank, head), F32),
        ),
        in_specs=[hbm] * 4 + [vmem],
        out_specs=(hbm, hbm, vmem),
        scratch_shapes=[
            pltpu.VMEM((tokens, head), BF16),
            pltpu.VMEM((width, head), BF16),
            pltpu.VMEM((width, head), BF16),
            pltpu.VMEM((NC, tokens, ck), BF16),
            pltpu.VMEM((width, head), F32),
            pltpu.VMEM((width, head), BF16),
            pltpu.VMEM((NC, NY, py, head), BF16),
            pltpu.VMEM((NC, NY - 1, py, head), BF16),
            pltpu.VMEM((NC, py, head), F32),
            pltpu.VMEM((NC, py, head), BF16),
            pltpu.VMEM((NC, NZ - 1, pz, head), BF16),
            pltpu.VMEM((head, head), F32),
            pltpu.VMEM((tokens, width), BF16),
            pltpu.VMEM((NX, rows, width), BF16),
            pltpu.VMEM((NX - 1, rows, width), BF16),
            pltpu.VMEM((NX - 1, rows, width), BF16),
            pltpu.VMEM((rows, width), F32),
            pltpu.VMEM((rows, width), BF16),
            pltpu.VMEM((width, head), BF16),
            dma((1 + width // 512,)),
            dma((3,)), pltpu.SemaphoreType.REGULAR((3,)),
            dma((NC, 4)), dma((NC, 4)),
            dma((NC, NX)), dma((NC, NX)),
            dma((NC, NY - 1)), dma((NC, NY - 1)),
            dma((NC,)), dma((NC,)),
            dma((NC,)), dma((NC,)),
            dma((NC, NY - 1)), dma((NC, NY - 1)),
            dma((NX,)), dma((NX,)),
            dma((NX - 1,)), dma((NX - 1,)),
            dma((NC,)),
        ],
        compiler_params=pltpu.CompilerParams(
            collective_id=0, has_side_effects=True, vmem_limit_bytes=56 * 2**20
        ),
        name="value_backward",
    )(layer_input, value_grad, value_weight, error_buffer, query_basis.T)
    input_grad, error_new, query_new = deliver(input_grad, error_new, query_new)
    return (input_grad, error_new, query_new.T)


def solution(mesh):
    return jax.shard_map(
        per_device,
        mesh=mesh,
        in_specs=(
            P(("dp", "tensor"), None),
            P("dp", "tensor"),
            P(None, "tensor"),
            P("dp", "tensor"),
            P("tensor", None),
        ),
        out_specs=(P(("dp", "tensor"), None), P("dp", "tensor"), P("tensor", None)),
        check_vma=False,
    )
```

time: 102 us -> 74.7 us (0.73)
  between operations: 14.1 us -> 0.64 us
  Pallas kernels: 81.9 us -> 73.8 us
  matrix products: 3.52 us -> 0 us
  local copies, waits for them, and re-layouts: 1.95 us -> 0 us
    pallas_call x2, Pallas kernels: 81.9 us -> 73.8 us  [the longest x1 71.4 us: per_device(): pl.pallas_call(kernel, out_shape=(jax.ShapeDtypeStruct((rows, width), BF1...]
    dot_general x1 -> x0, matrix products: 3.52 us -> none  [per_device(): lax.dot_general(value_grad, value_weight, (((1,), (1,)), ((), ())), prefe...]
    unnamed x12 -> x0, local copies, waits for them, and re-layouts: 1.95 us -> none
  transfers between devices with their start and end apart: 1 -> 0, of which waited for: 0 -> 0; matrix products, arithmetic and copies ran while one was open for 1% -> 0% of each run, Pallas kernels for 81% -> 0%
where the time goes in v2:
time: 74.7 us; the launch traced here: 74.5 us
  Pallas kernels  73.8 us (99%)
    pallas_call x1, Pallas kernels, per_device(): pl.pallas_call(kernel, out_shape=(jax.ShapeDtypeStruct((rows, width), BF1...  71.4 us
    pallas_call x1, Pallas kernels, deliver(): pl.pallas_call(deliver_kernel, out_shape=tuple((jax.ShapeDtypeStruct(a.sh...  2.48 us

profile of v2, /device:TPU:1, one launch (start us, length us, event | category | flops | bytes accessed | tf_op | source)
XLA Modules:
  0.0 74.5 jit_solution(8330730120922528136)
XLA Ops:
  0.6 71.4 %value_backward.1 = (bf16[48,4096]{1,0:T(8,128)(2,1)}, bf16[4096,128]{1,0:T(8,128)(2,1)}, f32[32,128]{1,0:T(8,128)}) custom-call(bf16[48,4096]{1,0:T(8,128)(2,1)} %x_hbm.1, bf16[384,128]{1,0:T(8,128)(2,1)} %g_hbm.1, bf16[4096,128]{1,0:T(8,128)(2,1)} %w_hbm.1, bf16[4096,128]{1,0:T(8,128)(2,1)} %e_hbm.1, f32[32,128]{1,0:T(8,128)} %bitcast.2), custom_call_target="tpu_custom_call" | custom-call | tf_op jit(solution)/shard_map/value_backward/pallas_call | solution.py:348
  72.0 2.5 %deliver.1 = (bf16[48,4096]{1,0:T(8,128)(2,1)}, bf16[4096,128]{1,0:T(8,128)(2,1)}, f32[32,128]{1,0:T(8,128)}) custom-call(bf16[48,4096]{1,0:T(8,128)(2,1)} %get-tuple-element.9.refs_0_, bf16[4096,128]{1,0:T(8,128)(2,1)} %get-tuple-element.10.refs_1_, f32[32,128]{1,0:T(8,128)} %get-tuple-element.11.refs_2_), custom_call_target="tpu_custom_call" | custom-call | tf_op jit(solution)/shard_map/deliver/pallas_call | solution.py:328

commit v3 on v2

--- a/solution.py
+++ b/solution.py
@@ -108,8 +108,8 @@
     def row_block(ref, owner):
         return ref.at[pl.ds(pl.multiple_of(owner * rows, rows), rows)]
 
-    def head_term(c):
-        if c == 0:
+    def head_term(i):
+        if i == 0:
             loads[1].wait()
 
         def tile(j, carry):
@@ -119,11 +119,11 @@
             ).astype(BF16)
             return carry
 
-        half = width // wide // 2
-        lax.fori_loop(c * half, (c + 1) * half, tile, 0)
-        if c == 0:
-            return
-        for d in range(NX):
+        quarter = width // wide // 4
+        lax.fori_loop(i * quarter, (i + 1) * quarter, tile, 0)
+
+    def term_send(i):
+        for d in (1, 3, 2, 0):
             remote(
                 row_block(term, owner_x(d, 1 - core)), other.at[d],
                 t_send.at[d], t_recv.at[d], sibling,
@@ -160,21 +160,19 @@
         for d in range(NX):
             wait_bytes(block(c, t), c_recv.at[c, d])
 
-        def tile(j, carry):
+        for d in (1, 3, 2, 0):
+            j = lax.rem(y + d, NY)
             off = pl.multiple_of(j * py, py)
             at = pl.multiple_of(c * ck + j * py, py)
             m = dot_rows(xg[c, :, pl.ds(off, py)], g_ref[...])
             m = m + e_ref[pl.ds(at, py), :].astype(F32)
             mom_ref[pl.ds(at, py), :] = m
-            ystage[c, j] = m.astype(BF16)
-            return carry
-
-        lax.fori_loop(0, NY, tile, 0)
-        for d in (1, 3, 2):
-            remote(
-                ystage.at[c, lax.rem(y + d, NY)], yrecv.at[c, d - 1],
-                ys_send.at[c, d - 1], ys_recv.at[c, d - 1], at_y(d),
-            )
+            if d > 0:
+                ystage[c, d - 1] = m.astype(BF16)
+                remote(
+                    ystage.at[c, d - 1], yrecv.at[c, d - 1],
+                    ys_send.at[c, d - 1], ys_recv.at[c, d - 1], at_y(d),
+                )
 
     def z_scatter(c):
         for d in range(1, NY):
@@ -193,6 +191,8 @@
                 device_id=at_z(d), device_id_type=MESH,
             ).start()
 
+    group = NZ // 4
+
     def z_gather(c):
         wait_bytes(zrecv.at[c], zs_recv.at[c])
         total = zsum[c, pl.ds(pl.multiple_of(z * pz, pz), pz), :]
@@ -201,47 +201,50 @@
         at = pl.multiple_of(c * ck + y * py + z * pz, pz)
         mine = mean_ref.at[pl.ds(at, pz)]
         mine[...] = (total * (1.0 / (NY * NZ))).astype(BF16)
-
         for d in FAR_FIRST:
+            ahead = lax.rem(z // group + 4 - lax.rem(z + d, NZ) // group, 4)
             pltpu.make_async_remote_copy(
-                mine, mine, zg_send.at[c], zg_recv.at[c],
+                mine, mine, zg_send.at[c], zg_recv.at[c, ahead],
                 device_id=at_z(d), device_id_type=MESH,
             ).start()
 
     def y_gather(c):
-        at = pl.multiple_of(c * ck + y * py, py)
-        wait_bytes(mean_ref.at[pl.ds(at, py - pz)], zg_recv.at[c])
-        mine = mean_ref.at[pl.ds(at, py)]
-        for d in (1, 3, 2):
-            remote(mine, mine, yg_send.at[c, d - 1], yg_recv.at[c, d - 1], at_y(d))
+        for d in (0, 1, 3, 2):
+            owner = lax.rem(z // group + d, 4)
+            at = pl.multiple_of(c * ck + y * py + owner * group * pz, pz)
+            come = group * pz - (pz if d == 0 else 0)
+            wait_bytes(mean_ref.at[pl.ds(at, come)], zg_recv.at[c, d])
+            mine = mean_ref.at[pl.ds(at, group * pz)]
+            for dy in (2, 1, 3):
+                pltpu.make_async_remote_copy(
+                    mine, mine, yg_send.at[c], yg_recv.at[c],
+                    device_id=at_y(dy), device_id_type=MESH,
+                ).start()
 
     def gram(c):
-        at = pl.multiple_of(c * ck + y * py, py)
-        for d in range(1, NY):
-            wait_bytes(mean_ref.at[pl.ds(at, py)], yg_recv.at[c, d - 1])
-        m = mean_ref[pl.ds(c * ck, ck), :]
-        part = dot_rows(m, m)
-        gram_ref[...] = part if c == 0 else gram_ref[...] + part
-
-    def pair_sum(c):
-        for d in range(NX):
-            wait_bytes(other.at[d], t_recv.at[d])
-        for d in range(NX):
-            mine = row_block(term, owner_x(d, core))
-
-            def tile(j, carry):
-                at = pl.ds(pl.multiple_of(j * wide, wide), wide)
-                both = mine[:, at].astype(F32) + other[d, :, at].astype(F32)
-                if d == 0:
-                    home[:, at] = both
-                else:
-                    pair[d - 1, :, at] = both.astype(BF16)
-                return carry
-
-            lax.fori_loop(0, width // wide, tile, 0)
-
-    def pair_send(c):
-        for d in (1, 3, 2):
+        def add(rows_at, first):
+            m = mean_ref[rows_at, :]
+            part = dot_rows(m, m)
+            gram_ref[...] = part if first else gram_ref[...] + part
+
+        wait_bytes(mean_ref.at[pl.ds(0, (NY - 1) * py)], yg_recv.at[c])
+        add(pl.ds(c * ck, ck), c == 0)
+
+    def pair_sum(d):
+        wait_bytes(other.at[d], t_recv.at[d])
+        mine = row_block(term, owner_x(d, core))
+
+        def tile(j, carry):
+            at = pl.ds(pl.multiple_of(j * wide, wide), wide)
+            both = mine[:, at].astype(F32) + other[d, :, at].astype(F32)
+            if d == 0:
+                home[:, at] = both
+            else:
+                pair[d - 1, :, at] = both.astype(BF16)
+            return carry
+
+        lax.fori_loop(0, width // wide, tile, 0)
+        if d > 0:
             remote(pair.at[d - 1], pair_recv.at[d - 1], p_send.at[d - 1], p_recv.at[d - 1], at_x(d))
 
     stores = []
@@ -266,15 +269,25 @@
         lax.fori_loop(0, width // wide, tile, 0)
         store(ig_ref, ig_hbm)
 
+    def drain(c):
+        while sends:
+            sends.pop().wait_send()
+
+    def drain_z(c):
+        for c in range(NC):
+            wait_bytes(zrecv.at[c], zs_send.at[c])
+
     stages = [
         (forward, 4.5), (forward_far, 8.7), (moment, 9.7), (z_scatter, 15.2), (z_gather, 24.0),
         (y_gather, 33.5), (gram, 39.0),
     ]
     order = [(2.6 * c + at, i, c, fn) for i, (fn, at) in enumerate(stages) for c in range(NC)]
     order += [
-        (0.0, 0, 0, greet), (18.0, 0, 0, head_term), (3.0, 0, 1, greet), (18.5, 0, 1, head_term),
-        (6.0, 0, 2, greet), (13.0, 0, 3, greet),
-        (21.0, 9, 0, pair_sum), (21.1, 9, 0, pair_send), (40.0, 9, 0, input_grad),
+        (0.0, 0, 0, greet), (3.0, 0, 1, greet), (6.0, 0, 2, greet), (13.0, 0, 3, greet),
+        (16.0, 9, 0, head_term), (18.6, 9, 1, head_term), (21.2, 9, 2, head_term), (23.1, 9, 3, head_term),
+        (23.2, 9, 0, term_send), (26.7, 9, 1, pair_sum), (29.3, 9, 3, pair_sum), (31.9, 9, 2, pair_sum),
+        (34.5, 9, 0, pair_sum), (47.0, 9, 0, input_grad), (46.0, 9, 0, drain_z),
+        (46.1, 9, 0, drain),
     ]
     for c in range(AHEAD):
         spread(c)
@@ -283,19 +296,26 @@
 
     q = q_ref[...]
     prod = high(q, gram_ref[...], ((1,), (0,)))
-    s = high(prod, q, ((1,), (1,)))
-    row_of = lax.broadcasted_iota(jnp.int32, (rank, 1), 0)
+    unit = lax.rsqrt(jnp.sum(prod * q, axis=1, keepdims=True))
+    q, prod = q * unit, prod * unit
+    s = high(prod, jnp.concatenate([q, jnp.zeros((head - rank, head), F32)], axis=0), ((1,), (1,)))
+    row_of = lax.broadcasted_iota(jnp.int32, (rank, head), 0)
     out = jnp.zeros((rank, head), F32)
-    for i in range(rank):
-        pivot = s[i:i + 1, i:i + 1]
-        inv = 1.0 / pivot
-        srow = s[i:i + 1, :] * inv
-        rrow = prod[i:i + 1, :] * inv
-        mine = row_of == i
-        out = jnp.where(mine, rrow * jnp.sqrt(pivot), out)
-        col = jnp.where(mine, 0.0, s[:, i:i + 1])
-        s = jnp.where(mine, srow, s - col * srow)
-        prod = jnp.where(mine, rrow, prod - col * rrow)
+    for i in range(0, rank, 2):
+        col0 = jnp.broadcast_to(s[:, i:i + 1], (rank, head))
+        col1 = jnp.broadcast_to(s[:, i + 1:i + 2], (rank, head))
+        a, b, d = col0[i:i + 1, :], col1[i:i + 1, :], col1[i + 1:i + 2, :]
+        det = a * d - b * b
+        inv = 1.0 / det
+        s0, s1 = s[i:i + 1, :], s[i + 1:i + 2, :]
+        p0, p1 = prod[i:i + 1, :], prod[i + 1:i + 2, :]
+        first, second = row_of == i, row_of == i + 1
+        out = jnp.where(first, p0 * lax.rsqrt(a), out)
+        out = jnp.where(second, (p1 - (b / a) * p0) * lax.rsqrt(det / a), out)
+        n0, n1 = (d * s0 - b * s1) * inv, (a * s1 - b * s0) * inv
+        s = jnp.where(first, n0, jnp.where(second, n1, s - col0 * n0 - col1 * n1))
+        n0, n1 = (d * p0 - b * p1) * inv, (a * p1 - b * p0) * inv
+        prod = jnp.where(first, n0, jnp.where(second, n1, prod - col0 * n0 - col1 * n1))
     qn_ref[...] = out
     b = high(q, prod, ((0,), (0,)))
     b_hi = b.astype(BF16)
@@ -310,26 +330,42 @@
 
     for cp in stores:
         cp.wait()
-    for cp in sends:
-        cp.wait_send()
+    drain(0)
     for c in range(NC):
-        wait_bytes(zrecv.at[c], zs_send.at[c])
         wait_bytes(zrecv.at[c], zg_send.at[c])
-
-
-def deliver_kernel(*refs):
-    n = len(refs) // 2
-    for src, dst in zip(refs[:n], refs[n:]):
-        dst[...] = src[...]
+        wait_bytes(mean_ref.at[pl.ds(0, (NY - 1) * py)], yg_send.at[c])
+
+
+def deliver_kernel(
+    ig_in, err_in, qn_in, ig_out, err_out, qn_out, ig_ref, err_ref, qn_ref, load_sem, store_sem
+):
+    n = load_sem.shape[0] - 2
+    tile = err_in.shape[0] // n
+    parts = [
+        (err_in.at[at], err_ref.at[at], err_out.at[at])
+        for at in (pl.ds(j * tile, tile) for j in range(n))
+    ] + [(ig_in, ig_ref, ig_out), (qn_in, qn_ref, qn_out)]
+    loads = [pltpu.make_async_copy(a, b, load_sem.at[i]) for i, (a, b, _) in enumerate(parts)]
+    stores = [pltpu.make_async_copy(b, c, store_sem.at[i]) for i, (_, b, c) in enumerate(parts)]
+    for cp in loads:
+        cp.start()
+    for load, out in zip(loads, stores):
+        load.wait()
+        out.start()
+    for cp in stores:
+        cp.wait()
 
 
 def deliver(*arrays):
-    vmem = pl.BlockSpec(memory_space=pltpu.VMEM)
+    hbm = pl.BlockSpec(memory_space=pl.ANY)
+    n = 4
     return pl.pallas_call(
         deliver_kernel,
         out_shape=tuple(jax.ShapeDtypeStruct(a.shape, a.dtype) for a in arrays),
-        in_specs=[vmem] * len(arrays),
-        out_specs=(vmem,) * len(arrays),
+        in_specs=[hbm] * len(arrays),
+        out_specs=(hbm,) * len(arrays),
+        scratch_shapes=[pltpu.VMEM(a.shape, a.dtype) for a in arrays]
+        + [pltpu.SemaphoreType.DMA((n + 2,))] * 2,
         compiler_params=pltpu.CompilerParams(vmem_limit_bytes=56 * 2**20),
         name="deliver",
     )(*arrays)
@@ -361,7 +397,7 @@
             pltpu.VMEM((NC, tokens, ck), BF16),
             pltpu.VMEM((width, head), F32),
             pltpu.VMEM((width, head), BF16),
-            pltpu.VMEM((NC, NY, py, head), BF16),
+            pltpu.VMEM((NC, NY - 1, py, head), BF16),
             pltpu.VMEM((NC, NY - 1, py, head), BF16),
             pltpu.VMEM((NC, py, head), F32),
             pltpu.VMEM((NC, py, head), BF16),
@@ -380,8 +416,8 @@
             dma((NC, NX)), dma((NC, NX)),
             dma((NC, NY - 1)), dma((NC, NY - 1)),
             dma((NC,)), dma((NC,)),
+            dma((NC,)), dma((NC, 4)),
             dma((NC,)), dma((NC,)),
-            dma((NC, NY - 1)), dma((NC, NY - 1)),
             dma((NX,)), dma((NX,)),
             dma((NX - 1,)), dma((NX - 1,)),
             dma((NC,)),

time: 74.7 us -> 70.2 us (0.940)
  Pallas kernels: 73.8 us -> 69 us
    pallas_call x1, Pallas kernels: 71.4 us -> 66.8 us  [per_device(): pl.pallas_call(kernel, out_shape=(jax.ShapeDtypeStruct((rows, width), BF1...]
where the time goes in v3:
time: 70.2 us; the launch traced here: 69.6 us
  Pallas kernels  69 us (98%)
    pallas_call x1, Pallas kernels, per_device(): pl.pallas_call(kernel, out_shape=(jax.ShapeDtypeStruct((rows, width), BF1...  66.8 us
    pallas_call x1, Pallas kernels, deliver(): pl.pallas_call(deliver_kernel, out_shape=tuple((jax.ShapeDtypeStruct(a.sh...  2.17 us

profile of v3, /device:TPU:1, one launch (start us, length us, event | category | flops | bytes accessed | tf_op | source)
XLA Modules:
  0.0 69.6 jit_solution(2071407720833178893)
XLA Ops:
  0.6 66.8 %value_backward.1 = (bf16[48,4096]{1,0:T(8,128)(2,1)}, bf16[4096,128]{1,0:T(8,128)(2,1)}, f32[32,128]{1,0:T(8,128)}) custom-call(bf16[48,4096]{1,0:T(8,128)(2,1)} %x_hbm.1, bf16[384,128]{1,0:T(8,128)(2,1)} %g_hbm.1, bf16[4096,128]{1,0:T(8,128)(2,1)} %w_hbm.1, bf16[4096,128]{1,0:T(8,128)(2,1)} %e_hbm.1, f32[32,128]{1,0:T(8,128)} %bitcast.2), custom_call_target="tpu_custom_call" | custom-call | tf_op jit(solution)/shard_map/value_backward/pallas_call | solution.py:384
  67.4 2.2 %deliver.1 = (bf16[48,4096]{1,0:T(8,128)(2,1)}, bf16[4096,128]{1,0:T(8,128)(2,1)}, f32[32,128]{1,0:T(8,128)}) custom-call(bf16[48,4096]{1,0:T(8,128)(2,1)} %get-tuple-element.9.ig_in, bf16[4096,128]{1,0:T(8,128)(2,1)} %get-tuple-element.10.err_in, f32[32,128]{1,0:T(8,128)} %get-tuple-element.11.qn_in), custom_call_target="tpu_custom_call" | custom-call | tf_op jit(solution)/shard_map/deliver/pallas_call | solution.py:362

commit v4 on v3

--- a/solution.py
+++ b/solution.py
@@ -277,22 +277,20 @@
         for c in range(NC):
             wait_bytes(zrecv.at[c], zs_send.at[c])
 
-    stages = [
-        (forward, 4.5), (forward_far, 8.7), (moment, 9.7), (z_scatter, 15.2), (z_gather, 24.0),
-        (y_gather, 33.5), (gram, 39.0),
-    ]
-    order = [(2.6 * c + at, i, c, fn) for i, (fn, at) in enumerate(stages) for c in range(NC)]
-    order += [
-        (0.0, 0, 0, greet), (3.0, 0, 1, greet), (6.0, 0, 2, greet), (13.0, 0, 3, greet),
-        (16.0, 9, 0, head_term), (18.6, 9, 1, head_term), (21.2, 9, 2, head_term), (23.1, 9, 3, head_term),
-        (23.2, 9, 0, term_send), (26.7, 9, 1, pair_sum), (29.3, 9, 3, pair_sum), (31.9, 9, 2, pair_sum),
-        (34.5, 9, 0, pair_sum), (47.0, 9, 0, input_grad), (46.0, 9, 0, drain_z),
-        (46.1, 9, 0, drain),
-    ]
     for c in range(AHEAD):
         spread(c)
-    for _, _, c, fn in sorted(order, key=lambda e: e[:3]):
-        fn(c)
+    order = [
+        (greet, 0), (greet, 1), (forward, 0), (greet, 2), (forward, 1), (forward_far, 0),
+        (moment, 0), (forward, 2), (forward_far, 1), (moment, 1), (forward, 3), (greet, 3),
+        (forward_far, 2), (moment, 2), (z_scatter, 0), (forward_far, 3), (z_scatter, 1),
+        (moment, 3), (head_term, 0), (head_term, 1), (z_scatter, 2), (head_term, 2), (head_term, 3),
+        (term_send, 0), (z_scatter, 3), (pair_sum, 1), (z_gather, 0), (pair_sum, 3), (z_gather, 1),
+        (pair_sum, 2), (z_gather, 2), (pair_sum, 0), (z_gather, 3), (y_gather, 0), (y_gather, 1),
+        (y_gather, 2), (y_gather, 3), (gram, 0), (gram, 1), (gram, 2), (drain_z, 0), (drain, 0),
+        (input_grad, 0), (gram, 3),
+    ]
+    for stage, c in order:
+        stage(c)
 
     q = q_ref[...]
     prod = high(q, gram_ref[...], ((1,), (0,)))

time: 70.2 us -> 69.6 us (level)
  no operation moved by 1% of the time
where the time goes in v4:
time: 69.6 us; the launch traced here: 69 us
  Pallas kernels  68.3 us (98%)
    pallas_call x1, Pallas kernels, per_device(): pl.pallas_call(kernel, out_shape=(jax.ShapeDtypeStruct((rows, width), BF1...  66.2 us
    pallas_call x1, Pallas kernels, deliver(): pl.pallas_call(deliver_kernel, out_shape=tuple((jax.ShapeDtypeStruct(a.sh...  2.17 us

profile of v4, /device:TPU:1, one launch (start us, length us, event | category | flops | bytes accessed | tf_op | source)
XLA Modules:
  0.0 69.0 jit_solution(8716219232748508073)
XLA Ops:
  0.6 66.2 %value_backward.1 = (bf16[48,4096]{1,0:T(8,128)(2,1)}, bf16[4096,128]{1,0:T(8,128)(2,1)}, f32[32,128]{1,0:T(8,128)}) custom-call(bf16[48,4096]{1,0:T(8,128)(2,1)} %x_hbm.1, bf16[384,128]{1,0:T(8,128)(2,1)} %g_hbm.1, bf16[4096,128]{1,0:T(8,128)(2,1)} %w_hbm.1, bf16[4096,128]{1,0:T(8,128)(2,1)} %e_hbm.1, f32[32,128]{1,0:T(8,128)} %bitcast.2), custom_call_target="tpu_custom_call" | custom-call | tf_op jit(solution)/shard_map/value_backward/pallas_call | solution.py:382
  66.8 2.2 %deliver.1 = (bf16[48,4096]{1,0:T(8,128)(2,1)}, bf16[4096,128]{1,0:T(8,128)(2,1)}, f32[32,128]{1,0:T(8,128)}) custom-call(bf16[48,4096]{1,0:T(8,128)(2,1)} %get-tuple-element.9.ig_in, bf16[4096,128]{1,0:T(8,128)(2,1)} %get-tuple-element.10.err_in, f32[32,128]{1,0:T(8,128)} %get-tuple-element.11.qn_in), custom_call_target="tpu_custom_call" | custom-call | tf_op jit(solution)/shard_map/deliver/pallas_call | solution.py:360

commit v5 on v4

--- a/solution.py
+++ b/solution.py
@@ -28,9 +28,9 @@
 
 
 def kernel(
-    x_hbm, g_hbm, w_hbm, e_hbm, q_ref,
-    ig_hbm, err_hbm, qn_ref,
-    g_ref, w_ref, e_ref,
+    x_hbm, g_hbm, w_hbm, e_hbm, q_hbm,
+    ig_hbm, err_hbm, qn_hbm,
+    g_ref, w_ref, e_ref, q_ref, qn_ref,
     xg, mom_ref, mean_ref, ystage, yrecv, zsum, zstage, zrecv, gram_ref,
     term, other, pair, pair_recv, home, ig_ref, err_ref,
     out_sem, load_sem, entered,
@@ -42,7 +42,7 @@
     x, core = t // NCORE, lax.rem(t, NCORE)
     rows, width = x_hbm.shape
     tokens, head = g_hbm.shape
-    rank = q_ref.shape[0]
+    rank = q_hbm.shape[0]
     ck = width // NC
     py = ck // NY
     pz = py // NZ
@@ -69,7 +69,7 @@
 
     loads = [
         pltpu.make_async_copy(src, dst, load_sem.at[i])
-        for i, (src, dst) in enumerate(((g_hbm, g_ref), (w_hbm, w_ref), (e_hbm, e_ref)))
+        for i, (src, dst) in enumerate(((g_hbm, g_ref), (w_hbm, w_ref), (e_hbm, e_ref), (q_hbm, q_ref)))
     ]
     for cp in loads:
         cp.start()
@@ -292,6 +292,7 @@
     for stage, c in order:
         stage(c)
 
+    loads[3].wait()
     q = q_ref[...]
     prod = high(q, gram_ref[...], ((1,), (0,)))
     unit = lax.rsqrt(jnp.sum(prod * q, axis=1, keepdims=True))
@@ -315,6 +316,7 @@
         n0, n1 = (d * p0 - b * p1) * inv, (a * p1 - b * p0) * inv
         prod = jnp.where(first, n0, jnp.where(second, n1, prod - col0 * n0 - col1 * n1))
     qn_ref[...] = out
+    store(qn_ref, qn_hbm)
     b = high(q, prod, ((0,), (0,)))
     b_hi = b.astype(BF16)
     b_both = jnp.concatenate([b_hi, (b - b_hi.astype(F32)).astype(BF16)], axis=0)
@@ -377,7 +379,6 @@
     py = ck // NY
     pz = py // NZ
     dma = pltpu.SemaphoreType.DMA
-    vmem = pl.BlockSpec(memory_space=pltpu.VMEM)
     hbm = pl.BlockSpec(memory_space=pltpu.HBM)
     input_grad, error_new, query_new = pl.pallas_call(
         kernel,
@@ -386,12 +387,14 @@
             jax.ShapeDtypeStruct((width, head), BF16),
             jax.ShapeDtypeStruct((rank, head), F32),
         ),
-        in_specs=[hbm] * 4 + [vmem],
-        out_specs=(hbm, hbm, vmem),
+        in_specs=[hbm] * 5,
+        out_specs=(hbm, hbm, hbm),
         scratch_shapes=[
             pltpu.VMEM((tokens, head), BF16),
             pltpu.VMEM((width, head), BF16),
             pltpu.VMEM((width, head), BF16),
+            pltpu.VMEM((rank, head), F32),
+            pltpu.VMEM((rank, head), F32),
             pltpu.VMEM((NC, tokens, ck), BF16),
             pltpu.VMEM((width, head), F32),
             pltpu.VMEM((width, head), BF16),
@@ -408,8 +411,8 @@
             pltpu.VMEM((rows, width), F32),
             pltpu.VMEM((rows, width), BF16),
             pltpu.VMEM((width, head), BF16),
-            dma((1 + width // 512,)),
-            dma((3,)), pltpu.SemaphoreType.REGULAR((3,)),
+            dma((2 + width // 512,)),
+            dma((4,)), pltpu.SemaphoreType.REGULAR((3,)),
             dma((NC, 4)), dma((NC, 4)),
             dma((NC, NX)), dma((NC, NX)),
             dma((NC, NY - 1)), dma((NC, NY - 1)),

time: 69.6 us -> 68.4 us (0.983)
  Pallas kernels: 68.3 us -> 67.2 us
    pallas_call x1, Pallas kernels: 66.2 us -> 65 us  [per_device(): pl.pallas_call(kernel, out_shape=(jax.ShapeDtypeStruct((rows, width), BF1...]
where the time goes in v5:
time: 68.4 us; the launch traced here: 67.8 us
  Pallas kernels  67.2 us (98%)
    pallas_call x1, Pallas kernels, per_device(): pl.pallas_call(kernel, out_shape=(jax.ShapeDtypeStruct((rows, width), BF1...  65 us
    pallas_call x1, Pallas kernels, deliver(): pl.pallas_call(deliver_kernel, out_shape=tuple((jax.ShapeDtypeStruct(a.sh...  2.17 us

profile of v5, /device:TPU:1, one launch (start us, length us, event | category | flops | bytes accessed | tf_op | source)
XLA Modules:
  0.0 67.8 jit_solution(18243694494275848307)
XLA Ops:
  0.6 65.0 %value_backward.1 = (bf16[48,4096]{1,0:T(8,128)(2,1)}, bf16[4096,128]{1,0:T(8,128)(2,1)}, f32[32,128]{1,0:T(8,128)}) custom-call(bf16[48,4096]{1,0:T(8,128)(2,1)} %x_hbm.1, bf16[384,128]{1,0:T(8,128)(2,1)} %g_hbm.1, bf16[4096,128]{1,0:T(8,128)(2,1)} %w_hbm.1, bf16[4096,128]{1,0:T(8,128)(2,1)} %e_hbm.1, f32[32,128]{1,0:T(8,128)} %bitcast.2), custom_call_target="tpu_custom_call" | custom-call | tf_op jit(solution)/shard_map/value_backward/pallas_call | solution.py:383
  65.6 2.2 %deliver.1 = (bf16[48,4096]{1,0:T(8,128)(2,1)}, bf16[4096,128]{1,0:T(8,128)(2,1)}, f32[32,128]{1,0:T(8,128)}) custom-call(bf16[48,4096]{1,0:T(8,128)(2,1)} %get-tuple-element.9.ig_in, bf16[4096,128]{1,0:T(8,128)(2,1)} %get-tuple-element.10.err_in, f32[32,128]{1,0:T(8,128)} %get-tuple-element.11.qn_in), custom_call_target="tpu_custom_call" | custom-call | tf_op jit(solution)/shard_map/deliver/pallas_call | solution.py:362
